TPU v7x, 32 devices: a whole 2x2x4 slice. The times are simulated.
32 devices in a mesh: pair: 4 (over z), dof: 8 (over y, x, core).
Axes of the slice: x: 2, y: 2, z: 4, core: 2. Of those that a mesh axis runs over, the one named last changes fastest.
Arguments:
- snapshots: float32 [128, 65536], P('pair', 'dof'), may hold values from -600 to 600
Outputs:
- rotated: float32 [128, 65536], P('pair', 'dof')
All inputs are finite; a program needn't handle non-finite values.
Results may differ from a plain program's by a relative error of at most 0.0003.
Values sent between devices are 32-bit elements; how exact they have to be, the bound alone decides.
A program may use at most 64 MiB of HBM per device.

v0:
```python
import jax
import jax.numpy as jnp
from jax import lax
from jax.sharding import PartitionSpec as P

STEPS = 4
SWEEPS = 2


highest = lax.Precision.HIGHEST


def passed_along(block, axis, distance):
    devices = range(lax.axis_size(axis))
    route = [(i - distance, i) for i in devices if i - distance in devices]
    return lax.ppermute(block, axis, route)


def jacobi(gram_matrix):
    pair_order = gram_matrix.shape[0]
    circle_size = pair_order - 1
    index_row = lax.broadcasted_iota(jnp.int32, (pair_order, pair_order), 0)
    index_col = lax.broadcasted_iota(jnp.int32, (pair_order, pair_order), 1)
    identity_mask = index_row == index_col
    upper_side = index_row < index_col
    indices = jnp.arange(pair_order, dtype=jnp.int32)

    def one_round(round_index, carried):
        gram_now, basis = carried
        shifted = (round_index % circle_size).astype(jnp.int32)
        mirror = (2 * shifted - indices + 2 * circle_size) % circle_size
        partner = jnp.where(
            indices == circle_size, shifted, jnp.where(indices == shifted, circle_size, mirror)
        )
        partner_mask = index_col == partner[:, None]
        zeros = jnp.zeros_like(gram_now)
        upper_part = jnp.where(upper_side, gram_now, gram_now.T)
        coupling = jnp.sum(jnp.where(partner_mask, upper_part, zeros), axis=1)
        own_diag = jnp.sum(jnp.where(identity_mask, gram_now, zeros), axis=1)
        other_diag = jnp.sum(jnp.where(partner_mask, own_diag[None, :] + zeros, zeros), axis=1)
        is_lower = indices < partner
        diag_lower = jnp.where(is_lower, own_diag, other_diag)
        diag_upper = jnp.where(is_lower, other_diag, own_diag)
        spread_diag = diag_upper - diag_lower
        orient = jnp.where(spread_diag >= 0, 1.0, -1.0).astype(jnp.float32)
        tangent = (
            orient
            * 2.0
            * coupling
            / (
                jnp.abs(spread_diag)
                + jnp.sqrt(spread_diag * spread_diag + 4.0 * coupling * coupling)
            )
        )
        cosine = 1.0 / jnp.sqrt(1.0 + tangent * tangent)
        sine_part = cosine * tangent
        signed_sine = jnp.where(is_lower, sine_part, -sine_part)
        rotation = jnp.where(
            identity_mask,
            cosine[:, None] + zeros,
            jnp.where(partner_mask, signed_sine[:, None] + zeros, zeros),
        )
        gram_now = jnp.dot(
            jnp.dot(rotation.T, gram_now, precision=highest), rotation, precision=highest
        )
        basis = jnp.dot(basis, rotation, precision=highest)
        return (gram_now, basis)

    start = (gram_matrix, jnp.eye(pair_order, dtype=jnp.float32))
    final_gram, basis = lax.fori_loop(0, SWEEPS * circle_size, one_round, start)
    return basis


def body(snapshots):
    pair_order = snapshots.shape[0]
    half_order = pair_order // 2
    device_place = lax.axis_index("pair")
    final_place = lax.axis_size("pair") - 1
    is_first = device_place == 0
    is_last = device_place == final_place
    pair_rows = snapshots
    for step_index in range(STEPS):
        local_gram = jnp.dot(pair_rows, pair_rows.T, precision=highest)
        gram_matrix = lax.psum(local_gram, "dof")
        turned = jacobi(gram_matrix)
        moved = jnp.dot(turned.T, pair_rows, precision=highest)
        new_top = moved[:half_order]
        new_low = moved[half_order:]
        rising = jnp.where(is_first, new_low, new_top)
        got_rising = passed_along(rising, "pair", 1)
        got_falling = passed_along(new_low, "pair", -1)
        next_top = jnp.where(is_first, new_top, got_rising)
        next_low = jnp.where(is_last, new_top, got_falling)
        pair_rows = jnp.concatenate([next_top, next_low], axis=0)
    return pair_rows


def solution(mesh):
    in_specs = (P("pair", "dof"),)
    out_specs = P("pair", "dof")
    return jax.shard_map(body, mesh=mesh, in_specs=in_specs, out_specs=out_specs, check_vma=False)
```

profile of v0, /device:TPU:0, one launch (start us, length us, event | category | flops | bytes accessed | tf_op | source)
XLA Modules:
  0.0 519.9 jit_solution(5323736316995581943)
XLA Ops:
  2.2 25.5 %psum.28 = f32[32,32]{1,0:T(8,128)S(1)} all-reduce(f32[32,32]{1,0:T(8,128)S(1)} %fusion.185), channel_id=1, replica_groups=mesh['pair'=4,'dof'=8] {'dof'}, use_global_device_ids=true, to_apply=%region_0.0 | all-reduce | flops 1024 | bytes 8192 | tf_op jit(solution)/shard_map/psum | solution.py:84
  27.7 85.2 %while.76 = (s32[]{:T(128)}, f32[32,32]{1,0:T(8,128)S(1)}, f32[32,32]{0,1:T(8,128)S(1)}, s32[]{:T(128)}, s32[]{:T(128)}, /*index=5*/s32[]{:T(128)}, s32[]{:T(128)}) while((s32[]{:T(128)}, f32[32,32]{1,0:T(8,128)S(1)}, f32[32,32]{0,1:T(8,128)S(1)}, s32[]{:T(128)}, s32[]{:T(128)}, /*index=5*/s32[]{:T(128)}, ...), condition=%wide.region_5.6_spmd.clone.clone, body=%wide.region_1.5_spmd.clone.clone.sunk | while | flops 1205001 | bytes 52267 | solution.py:70
  112.9 1.0 fusion.186
  114.8 3.5 collective-permute-start
  118.3 1.3 collective-permute-start.1
  119.6 7.6 %collective-permute-done = f32[16,8192]{1,0:T(8,128)S(1)} collective-permute-done((f32[16,8192]{1,0:T(8,128)}, f32[16,8192]{1,0:T(8,128)S(1)}, u32[]{:S(2)}, u32[]{:S(2)}) %collective-permute-start) | collective-permute-done | bytes 524320 | tf_op jit(solution)/shard_map/ppermute | solution.py:16
  128.0 3.1 collective-permute-done.1
  131.2 1.1 slice_select_fusion.10
  133.3 24.1 %psum.29 = f32[32,32]{1,0:T(8,128)S(1)} all-reduce(f32[32,32]{1,0:T(8,128)S(1)} %fusion.173), channel_id=1, replica_groups=mesh['pair'=4,'dof'=8] {'dof'}, use_global_device_ids=true, to_apply=%region_6.7 | all-reduce | flops 1024 | bytes 8192 | tf_op jit(solution)/shard_map/psum | solution.py:84
  157.4 85.2 %while.77 = (s32[]{:T(128)}, f32[32,32]{1,0:T(8,128)S(1)}, f32[32,32]{0,1:T(8,128)S(1)}, s32[]{:T(128)}, s32[]{:T(128)}, /*index=5*/s32[]{:T(128)}, s32[]{:T(128)}) while((s32[]{:T(128)}, f32[32,32]{1,0:T(8,128)S(1)}, f32[32,32]{0,1:T(8,128)S(1)}, s32[]{:T(128)}, s32[]{:T(128)}, /*index=5*/s32[]{:T(128)}, ...), condition=%wide.region_11.12_spmd.clone.clone, body=%wide.region_7.11_spmd.clone.clone.sunk | while | flops 1205001 | bytes 52267 | solution.py:70
  242.6 1.0 fusion.172
  244.4 3.6 collective-permute-start.2
  248.1 1.3 collective-permute-start.3
  249.4 7.6 %collective-permute-done.2 = f32[16,8192]{1,0:T(8,128)S(1)} collective-permute-done((f32[16,8192]{1,0:T(8,128)}, f32[16,8192]{1,0:T(8,128)S(1)}, u32[]{:S(2)}, u32[]{:S(2)}) %collective-permute-start.2) | collective-permute-done | bytes 524320 | tf_op jit(solution)/shard_map/ppermute | solution.py:16
  257.8 3.1 collective-permute-done.3
  260.9 1.1 slice_select_fusion.7
  263.0 24.2 %psum.30 = f32[32,32]{1,0:T(8,128)S(1)} all-reduce(f32[32,32]{1,0:T(8,128)S(1)} %fusion.171), channel_id=1, replica_groups=mesh['pair'=4,'dof'=8] {'dof'}, use_global_device_ids=true, to_apply=%region_12.13 | all-reduce | flops 1024 | bytes 8192 | tf_op jit(solution)/shard_map/psum | solution.py:84
  287.2 85.2 %while.78 = (s32[]{:T(128)}, f32[32,32]{1,0:T(8,128)S(1)}, f32[32,32]{0,1:T(8,128)S(1)}, s32[]{:T(128)}, s32[]{:T(128)}, /*index=5*/s32[]{:T(128)}, s32[]{:T(128)}) while((s32[]{:T(128)}, f32[32,32]{1,0:T(8,128)S(1)}, f32[32,32]{0,1:T(8,128)S(1)}, s32[]{:T(128)}, s32[]{:T(128)}, /*index=5*/s32[]{:T(128)}, ...), condition=%wide.region_17.18_spmd.clone.clone, body=%wide.region_13.17_spmd.clone.clone.sunk | while | flops 1205001 | bytes 52267 | solution.py:70
  372.4 1.0 fusion.170
  374.3 3.6 collective-permute-start.4
  378.0 1.3 collective-permute-start.5
  379.3 7.6 %collective-permute-done.4 = f32[16,8192]{1,0:T(8,128)S(1)} collective-permute-done((f32[16,8192]{1,0:T(8,128)}, f32[16,8192]{1,0:T(8,128)S(1)}, u32[]{:S(2)}, u32[]{:S(2)}) %collective-permute-start.4) | collective-permute-done | bytes 524320 | tf_op jit(solution)/shard_map/ppermute | solution.py:16
  387.7 3.1 collective-permute-done.5
  390.8 1.1 slice_select_fusion.4
  392.9 24.2 %psum.31 = f32[32,32]{1,0:T(8,128)S(1)} all-reduce(f32[32,32]{1,0:T(8,128)S(1)} %fusion.169), channel_id=1, replica_groups=mesh['pair'=4,'dof'=8] {'dof'}, use_global_device_ids=true, to_apply=%region_18.19 | all-reduce | flops 1024 | bytes 8192 | tf_op jit(solution)/shard_map/psum | solution.py:84
  417.1 85.2 %while.79 = (s32[]{:T(128)}, f32[32,32]{1,0:T(8,128)S(1)}, f32[32,32]{0,1:T(8,128)S(1)}, s32[]{:T(128)}, s32[]{:T(128)}, /*index=5*/s32[]{:T(128)}, s32[]{:T(128)}) while((s32[]{:T(128)}, f32[32,32]{1,0:T(8,128)S(1)}, f32[32,32]{0,1:T(8,128)S(1)}, s32[]{:T(128)}, s32[]{:T(128)}, /*index=5*/s32[]{:T(128)}, ...), condition=%wide.region_23.24_spmd.clone.clone, body=%wide.region_19.23_spmd.clone.clone.sunk | while | flops 1205001 | bytes 52267 | solution.py:70
  502.3 1.0 fusion.168
  503.4 2.6 collective-permute-start.6
  506.1 1.3 collective-permute-start.7
  507.4 7.3 %collective-permute-done.6 = f32[16,8192]{1,0:T(8,128)S(1)} collective-permute-done((f32[16,8192]{1,0:T(8,128)S(1)}, f32[16,8192]{1,0:T(8,128)S(1)}, u32[]{:S(2)}, u32[]{:S(2)}) %collective-permute-start.6) | collective-permute-done | bytes 524320 | tf_op jit(solution)/shard_map/ppermute | solution.py:16
  514.7 4.1 collective-permute-done.7
  518.9 1.0 pad_maximum_fusion.3
  (2508 shorter events, 328.7 us)
Async XLA Ops:
  0.0 1.2 copy-start
  0.0 0.6 copy-start.1
  2.2 25.5 %copy-start.3 = (f32[32,32]{0,1:T(8,128)S(1)}, f32[32,32]{0,1:T(8,128)}, u32[]{:S(2)}) copy-start(f32[32,32]{0,1:T(8,128)} %copy-done.1) | copy-start | bytes 12292
  114.8 12.4 %collective-permute-start = (f32[16,8192]{1,0:T(8,128)}, f32[16,8192]{1,0:T(8,128)S(1)}, u32[]{:S(2)}, u32[]{:S(2)}) collective-permute-start(f32[16,8192]{1,0:T(8,128)} %get-tuple-element.955), channel_id=1, source_target_pairs={{0,8},{8,16},{16,24},{1,9},{9,17},{17,25},{2,10},{10,18},{18,26},{... | collective-permute-start | bytes 1572872 | tf_op jit(solution)/shard_map/ppermute | solution.py:16
  118.3 12.9 %collective-permute-start.1 = (f32[16,8192]{1,0:T(8,128)S(1)}, f32[16,8192]{1,0:T(8,128)}, u32[]{:S(2)}, u32[]{:S(2)}) collective-permute-start(f32[16,8192]{1,0:T(8,128)S(1)} %get-tuple-element.956), channel_id=1, source_target_pairs={{8,0},{16,8},{24,16},{9,1},{17,9},{25,17},{10,2},{18,10},{26,18},{... | collective-permute-start | bytes 1572872 | tf_op jit(solution)/shard_map/ppermute | solution.py:16
  127.2 0.8 copy-start.6
  133.3 24.1 %copy-start.4 = (f32[32,32]{0,1:T(8,128)S(1)}, f32[32,32]{0,1:T(8,128)}, u32[]{:S(2)}) copy-start(f32[32,32]{0,1:T(8,128)} %copy-done.1) | copy-start | bytes 12292
  244.4 12.6 %collective-permute-start.2 = (f32[16,8192]{1,0:T(8,128)}, f32[16,8192]{1,0:T(8,128)S(1)}, u32[]{:S(2)}, u32[]{:S(2)}) collective-permute-start(f32[16,8192]{1,0:T(8,128)} %get-tuple-element.951), channel_id=1, source_target_pairs={{0,8},{8,16},{16,24},{1,9},{9,17},{17,25},{2,10},{10,18},{18,26},{... | collective-permute-start | bytes 1572872 | tf_op jit(solution)/shard_map/ppermute | solution.py:16
  248.1 12.9 %collective-permute-start.3 = (f32[16,8192]{1,0:T(8,128)S(1)}, f32[16,8192]{1,0:T(8,128)}, u32[]{:S(2)}, u32[]{:S(2)}) collective-permute-start(f32[16,8192]{1,0:T(8,128)S(1)} %get-tuple-element.952), channel_id=1, source_target_pairs={{8,0},{16,8},{24,16},{9,1},{17,9},{25,17},{10,2},{18,10},{26,18},{... | collective-permute-start | bytes 1572872 | tf_op jit(solution)/shard_map/ppermute | solution.py:16
  257.0 0.8 copy-start.7
  263.0 24.2 %copy-start.5 = (f32[32,32]{0,1:T(8,128)S(1)}, f32[32,32]{0,1:T(8,128)}, u32[]{:S(2)}) copy-start(f32[32,32]{0,1:T(8,128)} %copy-done.1) | copy-start | bytes 12292
  374.3 12.6 %collective-permute-start.4 = (f32[16,8192]{1,0:T(8,128)}, f32[16,8192]{1,0:T(8,128)S(1)}, u32[]{:S(2)}, u32[]{:S(2)}) collective-permute-start(f32[16,8192]{1,0:T(8,128)} %get-tuple-element.947), channel_id=1, source_target_pairs={{0,8},{8,16},{16,24},{1,9},{9,17},{17,25},{2,10},{10,18},{18,26},{... | collective-permute-start | bytes 1572872 | tf_op jit(solution)/shard_map/ppermute | solution.py:16
  378.0 12.9 %collective-permute-start.5 = (f32[16,8192]{1,0:T(8,128)S(1)}, f32[16,8192]{1,0:T(8,128)}, u32[]{:S(2)}, u32[]{:S(2)}) collective-permute-start(f32[16,8192]{1,0:T(8,128)S(1)} %get-tuple-element.948), channel_id=1, source_target_pairs={{8,0},{16,8},{24,16},{9,1},{17,9},{25,17},{10,2},{18,10},{26,18},{... | collective-permute-start | bytes 1572872 | tf_op jit(solution)/shard_map/ppermute | solution.py:16
  386.9 0.8 copy-start.8
  392.9 24.2 %copy-start.2 = (f32[32,32]{0,1:T(8,128)S(1)}, f32[32,32]{0,1:T(8,128)}, u32[]{:S(2)}) copy-start(f32[32,32]{0,1:T(8,128)} %copy-done.1) | copy-start | bytes 12292
  503.4 11.2 %collective-permute-start.6 = (f32[16,8192]{1,0:T(8,128)S(1)}, f32[16,8192]{1,0:T(8,128)S(1)}, u32[]{:S(2)}, u32[]{:S(2)}) collective-permute-start(f32[16,8192]{1,0:T(8,128)S(1)} %get-tuple-element.943), channel_id=1, source_target_pairs={{0,8},{8,16},{16,24},{1,9},{9,17},{17,25},{2,10},{10,18},{18,26},{... | collective-permute-start | bytes 1572872 | tf_op jit(solution)/shard_map/ppermute | solution.py:16
  506.1 12.7 %collective-permute-start.7 = (f32[16,8192]{1,0:T(8,128)S(1)}, f32[16,8192]{1,0:T(8,128)S(1)}, u32[]{:S(2)}, u32[]{:S(2)}) collective-permute-start(f32[16,8192]{1,0:T(8,128)S(1)} %get-tuple-element.944), channel_id=1, source_target_pairs={{8,0},{16,8},{24,16},{9,1},{17,9},{25,17},{10,2},{18,10},{26,18},{... | collective-permute-start | bytes 1572872 | tf_op jit(solution)/shard_map/ppermute | solution.py:16
where the time goes:
time: 521 us; the launch traced here: 520 us
  matrix products  200 us (38%)
  other arithmetic  115 us (22%)
  blocking collectives  97.9 us (19%)
  waiting for transfers between devices  43.7 us (8%)
  loops' own time  22.4 us (4%)
  local copies, waits for them, and re-layouts  22.1 us (4%)
  starting transfers between devices  18.5 us (4%)
    psum x4, blocking collectives, body(): gram_matrix = lax.psum(local_gram, 'dof')  97.9 us
    dot_general x248, matrix products, one_round(): basis = jnp.dot(basis, rotation, precision=highest)  69.6 us
    dot_general x248, matrix products, one_round(): jnp.dot(rotation.T, gram_now, precision=highest)  69.6 us
    dot_general x248, matrix products, one_round(): jnp.dot(jnp.dot(rotation.T, gram_now, precision=highest), rotation, preci...  52.7 us
    reduce_sum x248, other arithmetic, one_round(): jnp.sum(jnp.where(partner_mask, own_diag[None, :] + zeros, zeros), axis=1)  44.4 us
    ppermute x8, waiting for transfers between devices, passed_along(): return lax.ppermute(block, axis, route)  43.7 us
    reduce_sum x248, other arithmetic, one_round(): own_diag = jnp.sum(jnp.where(identity_mask, gram_now, zeros), axis=1)  43.6 us
    another operation x4, loops' own time, jacobi(): final_gram, basis = lax.fori_loop(0, SWEEPS * circle_size, one_round, start)  22.4 us
  transfers between devices with their start and end apart: 8, of which 8 were waited for; matrix products, arithmetic and copies ran while one was open for 0% of the time, Pallas kernels for 0%

commit v1 on v0

v1 whole, which is shorter than its diff:
```python
import functools

import jax
import jax.numpy as jnp
from jax import lax
from jax.experimental import pallas as pl
from jax.experimental.pallas import tpu as pltpu
from jax.sharding import PartitionSpec as P

STEPS = 4
SWEEPS = 2
LANES = 128

highest = lax.Precision.HIGHEST


def dot(a, b, contract):
    return lax.dot_general(
        a, b, ((contract[:1], contract[1:]), ((), ())),
        precision=highest, preferred_element_type=jnp.float32,
    )


def natural_row(place, width, half, order):
    low = place >= width
    local = jnp.where(low, place - width, place)
    problem, k = local // half, local % half
    top_index = jnp.where(k == 0, order - 1, k)
    low_index = jnp.where(k == 0, 0, order - 1 - k)
    return problem * order + jnp.where(low, low_index, top_index), problem


def moved_from(row, half, order, pairs):
    pair, inner = row // order, row % order
    upper = inner < half
    offset = jnp.where(upper, inner, inner - half)
    up_pair = jnp.where(pair <= 1, 0, pair - 1)
    up_half = jnp.where(pair == 1, half, 0)
    last = pair == pairs - 1
    low_pair = jnp.where(last, pair, pair + 1)
    low_half = jnp.where(last, 0, half)
    return jnp.where(upper, up_pair, low_pair) * order + jnp.where(upper, up_half, low_half) + offset


def angles(a, b, c, threshold):
    d = b - a
    c2 = 2.0 * c
    square = d * d + c2 * c2
    big = 2.0 ** 64
    db, cb = d * big, c2 * big
    inverse = jnp.where(
        square < 1e-30, lax.rsqrt(db * db + cb * cb) * big, lax.rsqrt(square)
    )
    co_square = 0.5 + 0.5 * (jnp.abs(d) * inverse)
    root = lax.rsqrt(co_square)
    signed = jnp.where(d >= threshold, c, -c)
    return co_square * root, signed * inverse * root


def kernel(pairs, half, gram_ref, turn_ref):
    order = 2 * half
    circle = order - 1
    rows = pairs * order
    width = -(-pairs * half // LANES) * LANES
    groups = width // LANES
    two = 2 * width
    f32 = jnp.float32

    lane = lax.broadcasted_iota(jnp.int32, (half, LANES), 1)
    row = lax.broadcasted_iota(jnp.int32, (half, LANES), 0)
    k_lane = lane % half
    group_start = lane - k_lane
    diagonal = k_lane == row
    k0, kend = k_lane == 0, k_lane == half - 1
    r0, rend = row == 0, row == half - 1
    row_index = group_start + row
    lane_q = lax.broadcasted_iota(jnp.int32, (order, LANES), 1) % half
    row_q = lax.broadcasted_iota(jnp.int32, (order, LANES), 0)
    q0, qend = lane_q == 0, lane_q == half - 1

    place_c = lax.broadcasted_iota(jnp.int32, (rows, two), 1)
    nat_c, problem_c = natural_row(place_c, width, half, order)
    nat_r = lax.broadcasted_iota(jnp.int32, (rows, two), 0)
    used = problem_c < pairs
    enter = jnp.where(used & (nat_c == nat_r), 1.0, 0.0).astype(f32)
    moved_enter = jnp.where(
        used & (moved_from(nat_c, half, order, pairs) == nat_r), 1.0, 0.0
    ).astype(f32)
    move_row = lax.broadcasted_iota(jnp.int32, (rows, rows), 0)
    move_col = lax.broadcasted_iota(jnp.int32, (rows, rows), 1)
    move = jnp.where(
        moved_from(move_col, half, order, pairs) == move_row, 1.0, 0.0
    ).astype(f32)
    to_next = dot(enter, moved_enter, (0, 0))
    to_end = dot(enter, move, (0, 0))

    def column_shift(top, low, at0, atend):
        left = pltpu.roll(top, LANES - 1, 1)
        right = pltpu.roll(low, 1, 1)
        return (
            jnp.where(at0, top, jnp.where(atend, low, left)),
            jnp.where(at0, left, right),
        )

    def row_shift(top, low):
        up = pltpu.roll(top, half - 1, 0)
        down = pltpu.roll(low, 1, 0)
        return jnp.where(r0, top, jnp.where(rend, low, up)), jnp.where(r0, up, down)

    def one_round(r, states):
        m = r % circle
        t_index, b_index = (m + k_lane) % circle, (m - k_lane + circle) % circle
        swapped = k0 | (t_index > b_index)
        threshold = jnp.where(swapped, jnp.float32(1.2e-38), jnp.float32(0.0))
        out = []
        for aa, bb, ee, dd, qt, qb in states:
            def pick(x):
                s = jnp.sum(jnp.where(diagonal, x, 0.0), axis=0, keepdims=True)
                return jnp.broadcast_to(s, x.shape)

            co_j, si_j = angles(pick(aa), pick(dd), pick(bb), threshold)
            co_i = jnp.take_along_axis(co_j, row_index, axis=1)
            si_i = jnp.take_along_axis(si_j, row_index, axis=1)
            ac, ad = aa * co_j - bb * si_j, aa * si_j + bb * co_j
            ec, ed = ee * co_j - dd * si_j, ee * si_j + dd * co_j
            a1, e1 = co_i * ac - si_i * ec, si_i * ac + co_i * ec
            b1, d1 = co_i * ad - si_i * ed, si_i * ad + co_i * ed
            a2, e2 = row_shift(a1, e1)
            b2, d2 = row_shift(b1, d1)
            a3, b3 = column_shift(a2, b2, k0, kend)
            e3, d3 = column_shift(e2, d2, k0, kend)
            co_q = jnp.concatenate([co_j, co_j], axis=0)
            si_q = jnp.concatenate([si_j, si_j], axis=0)
            q1, q2 = column_shift(
                qt * co_q - qb * si_q, qt * si_q + qb * co_q, q0, qend
            )
            out.append((a3, b3, e3, d3, q1, q2))
        return tuple(out)

    def blocks(gram, g):
        def gather(first_row, first_col):
            total = jnp.zeros((half, LANES), f32)
            for p in range(min(LANES // half, pairs - g * (LANES // half))):
                at = first_row + g * LANES + p * half
                part = gram[at:at + half, first_col + g * LANES:first_col + (g + 1) * LANES]
                total = jnp.where(group_start == p * half, part, total)
            return total

        unused = (group_start // half + g * (LANES // half)) >= pairs
        spare = jnp.where(diagonal, (row + 1).astype(f32), 0.0)
        aa = jnp.where(unused, spare, gather(0, 0))
        bb = jnp.where(unused, 0.0, gather(0, width))
        ee = jnp.where(unused, 0.0, gather(width, 0))
        dd = jnp.where(unused, jnp.where(diagonal, spare + half, 0.0), gather(width, width))
        qt = jnp.where(row_q == lane_q, 1.0, 0.0).astype(f32)
        qb = jnp.where(row_q == lane_q + half, 1.0, 0.0).astype(f32)
        return aa, bb, ee, dd, qt, qb

    def spread(states):
        place_row = lax.broadcasted_iota(jnp.int32, (width, LANES), 0) // half
        place_lane = lax.broadcasted_iota(jnp.int32, (width, LANES), 1) // half
        columns = []
        for which in (4, 5):
            for g in range(groups):
                q = states[g][which]
                mine = place_row == place_lane + g * (LANES // half)
                parts = []
                for h in (0, 1):
                    part = q[h * half:(h + 1) * half]
                    tall = jnp.concatenate([part] * (width // half), axis=0)
                    parts.append(jnp.where(mine, tall, 0.0))
                columns.append(jnp.concatenate(parts, axis=0))
        return jnp.concatenate(columns, axis=1)

    gram = dot(enter, dot(gram_ref[...], enter, (1, 0)), (0, 0))
    total = None
    for step in range(STEPS):
        states = tuple(blocks(gram, g) for g in range(groups))
        states = lax.fori_loop(0, SWEEPS * circle, one_round, states)
        turn = dot(spread(states), to_next if step < STEPS - 1 else to_end, (1, 0))
        total = dot(enter, turn, (1, 0)) if total is None else dot(total, turn, (1, 0))
        if step < STEPS - 1:
            gram = dot(turn, dot(gram, turn, (1, 0)), (0, 0))
    turn_ref[...] = total.T


def body(snapshots):
    order, dofs = snapshots.shape
    pairs = lax.axis_size("pair")
    part = lax.all_to_all(snapshots, "pair", split_axis=1, concat_axis=0, tiled=True)
    gram = lax.psum(jnp.dot(part, part.T, precision=highest), ("pair", "dof"))
    everything = lax.all_gather(snapshots, "pair", axis=0, tiled=True)
    rows = pairs * order
    turn = pl.pallas_call(
        functools.partial(kernel, pairs, order // 2),
        out_shape=jax.ShapeDtypeStruct((rows, rows), jnp.float32),
        in_specs=[pl.BlockSpec(memory_space=pltpu.VMEM)],
        out_specs=pl.BlockSpec(memory_space=pltpu.VMEM),
        compiler_params=pltpu.CompilerParams(vmem_limit_bytes=32 * 2**20),
        cost_estimate=pl.CostEstimate(flops=10**9, bytes_accessed=10**8, transcendentals=0),
        name="rotations",
    )(gram)
    mine = lax.dynamic_slice_in_dim(turn, lax.axis_index("pair") * order, order, 0)
    return jnp.dot(mine, everything, precision=highest)


def solution(mesh):
    in_specs = (P("pair", "dof"),)
    out_specs = P("pair", "dof")
    return jax.shard_map(body, mesh=mesh, in_specs=in_specs, out_specs=out_specs, check_vma=False)
```

time: 521 us -> 287 us (0.55)
  matrix products: 200 us -> 7.01 us
  waiting for transfers between devices: 43.7 us -> 176 us
  other arithmetic: 115 us -> 0 us
  blocking collectives: 97.9 us -> 31.8 us
  Pallas kernels: 0 us -> 53.1 us
  loops' own time: 22.4 us -> 0 us
  local copies, waits for them, and re-layouts: 22.1 us -> 2.15 us
  starting transfers between devices: 18.5 us -> 0.05 us
  between operations: 0.24 us -> 14.9 us
    dot_general x752 -> x2, matrix products: 200 us -> 7.01 us  [the longest x1 5.4 us: body(): return jnp.dot(mine, everything, precision=highest)]
    psum x0 -> x1, waiting for transfers between devices: none -> 176 us  [body(): gram = lax.psum(jnp.dot(part, part.T, precision=highest), ('pair', 'dof'))]
    psum x4 -> x0, blocking collectives: 97.9 us -> none  [body(): gram_matrix = lax.psum(local_gram, 'dof')]
    reduce_sum x496 -> x0, other arithmetic: 88 us -> none  [the longest x248 44.4 us: one_round(): jnp.sum(jnp.where(partner_mask, own_diag[None, :] + zeros, zeros), axis=1)]
    pallas_call x0 -> x1, Pallas kernels: none -> 53.1 us  [body(): pl.pallas_call(functools.partial(kernel, pairs, order // 2), out_shape=ja...]
    ppermute x8 -> x0, waiting for transfers between devices: 43.7 us -> none  [passed_along(): return lax.ppermute(block, axis, route)]
    all_to_all x0 -> x1, blocking collectives: none -> 31.8 us  [body(): lax.all_to_all(snapshots, 'pair', split_axis=1, concat_axis=0, tiled=True)]
    another operation x4 -> x0, loops' own time: 22.4 us -> none  [jacobi(): final_gram, basis = lax.fori_loop(0, SWEEPS * circle_size, one_round, start)]
  transfers between devices with their start and end apart: 8 -> 2, of which waited for: 8 -> 1; matrix products, arithmetic and copies ran while one was open for 0% -> 0% of each run, Pallas kernels for 0% -> 19%
where the time goes in v1:
time: 287 us; the launch traced here: 285 us
  waiting for transfers between devices  176 us (61%)
  Pallas kernels  53.1 us (19%)
  blocking collectives  31.8 us (11%)
  between operations  14.9 us (5%)
  matrix products  7.01 us (2%)
    psum x1, waiting for transfers between devices, body(): gram = lax.psum(jnp.dot(part, part.T, precision=highest), ('pair', 'dof'))  176 us
    pallas_call x1, Pallas kernels, body(): pl.pallas_call(functools.partial(kernel, pairs, order // 2), out_shape=ja...  53.1 us
    all_to_all x1, blocking collectives, body(): lax.all_to_all(snapshots, 'pair', split_axis=1, concat_axis=0, tiled=True)  31.8 us
  transfers between devices with their start and end apart: 2, of which 1 were waited for; matrix products, arithmetic and copies ran while one was open for 0% of the time, Pallas kernels for 19%

profile of v1, /device:TPU:0, one launch (start us, length us, event | category | flops | bytes accessed | tf_op | source)
XLA Modules:
  0.0 285.5 jit_solution(14716894741876432060)
XLA Ops:
  7.4 0.0 all-reduce.2.cloned.1.call-start
  7.4 1.3 copy.6
  8.7 31.8 %all_to_all.19 = f32[32,4,2048]{2,0,1:T(8,128)S(1)} all-to-all(f32[32,4,2048]{2,0,1:T(8,128)S(1)} %bitcast.12), channel_id=1, replica_groups=mesh['pair'=4,'dof'=8] {'pair'}, dimensions={1} | all-to-all | bytes 2097152 | tf_op jit(solution)/shard_map/all_to_all | solution.py:190
  40.5 1.6 fusion.3
  42.2 0.0 all-reduce.2.cloned.1.call-update
  42.2 0.0 all-gather.2.cloned.1.call-start
  42.2 0.5 all-gather.2.cloned.1.call-update
  42.8 175.9 %all-reduce.2.cloned.1.call-done.gram_ref = f32[128,128]{1,0:T(8,128)} async-done(((f32[128,128]{1,0:T(8,128)}), f32[128,128]{1,0:T(8,128)}) %all-reduce.2.cloned.1.call-update) | async-done | bytes 65552 | tf_op jit(solution)/shard_map/psum | solution.py:191
  218.7 0.0 copy-start
  218.7 0.8 copy-done
  219.5 53.1 %rotations.1 = f32[128,128]{1,0:T(8,128)S(1)} custom-call(f32[128,128]{1,0:T(8,128)S(1)} %copy-done), custom_call_target="tpu_custom_call" | custom-call | flops 1000000000 | bytes 100000000 | tf_op jit(solution)/shard_map/rotations/pallas_call | solution.py:194
  272.6 0.0 all-gather.2.cloned.1.call-done
  272.6 5.4 %fusion = f32[32,8192]{1,0:T(8,128)} fusion(f32[128,8192]{1,0:T(8,128)} %all-gather.2.cloned.1.call-done, f32[128,128]{1,0:T(8,128)S(1)} %rotations.1, s32[]{:T(128)S(6)} %select_n.3), kind=kOutput, calls=%fused_computation.1 | convolution fusion | flops 402653184 | bytes 5259268 | tf_op jit(solution)/shard_map/dot_general | solution.py:204
Async XLA Ops:
  7.4 211.3 %all-reduce.2.cloned.1.call-start = ((), (), s32[]{:S(2)}) async-start(), calls=%async_computation.1 | async-start | bytes 131072 | tf_op jit(solution)/shard_map/psum | solution.py:191
  42.2 230.5 %all-gather.2.cloned.1.call-start = ((), (), s32[]{:S(2)}) async-start(), calls=%async_computation.2 | async-start | bytes 5242880 | tf_op jit(solution)/shard_map/all_gather | solution.py:192
  218.7 0.8 copy-start
Sparse Core Ops, SparseCore 0:
  42.3 176.3 all-reduce.1
Sparse Core Ops, SparseCore 1:
  44.2 80.0 all-gather.1

commit v2 on v1

--- a/solution.py
+++ b/solution.py
@@ -184,24 +184,160 @@
     turn_ref[...] = total.T
 
 
+def greet(pairs, dofs, pair, dof):
+    barrier = pltpu.get_barrier_semaphore()
+    for off in range(1, pairs):
+        pl.semaphore_signal(
+            barrier, inc=1, device_id=(lax.rem(pair + off, pairs), dof),
+            device_id_type=pl.DeviceIdType.MESH,
+        )
+    for off in range(1, dofs):
+        pl.semaphore_signal(
+            barrier, inc=1, device_id=(pair, lax.rem(dof + off, dofs)),
+            device_id_type=pl.DeviceIdType.MESH,
+        )
+    pl.semaphore_wait(barrier, pairs + dofs - 2)
+
+
+def send(src, dst, sems, off, device):
+    copy = pltpu.make_async_remote_copy(
+        src_ref=src, dst_ref=dst, send_sem=sems.at[0, off], recv_sem=sems.at[1, off],
+        device_id=device, device_id_type=pl.DeviceIdType.MESH,
+    )
+    copy.start()
+    return copy
+
+
+def gram_kernel(pairs, dofs, x_ref, part_ref, gram_ref, local, gathered, sums, crossed, whole,
+                sem_x, sem_scatter, sem_cross, sem_gather):
+    pair, dof = lax.axis_index("pair"), lax.axis_index("dof")
+    order = x_ref.shape[0]
+    quarter = part_ref.shape[1]
+    chunk = sums.shape[0]
+    greet(pairs, dofs, pair, dof)
+
+    def rows_of(place):
+        return pl.ds(pl.multiple_of(place * order, order), order)
+
+    def columns_of(place):
+        return pl.ds(pl.multiple_of(place * quarter, quarter), quarter)
+
+    copies = []
+    for off in range(pairs - 1, 0, -1):
+        peer = lax.rem(pair + off, pairs)
+        copies.append(send(
+            x_ref.at[:, columns_of(peer)], part_ref.at[rows_of(pair), :], sem_x, off, (peer, dof)
+        ))
+    part_ref[rows_of(pair), :] = x_ref[:, columns_of(pair)]
+    for copy in copies:
+        copy.wait()
+    part = part_ref[...]
+    local[...] = dot(part, part, (1, 1)).reshape(local.shape)
+
+    copies = []
+    for off in range(1, dofs):
+        peer = lax.rem(dof + off, dofs)
+        copies.append(send(local.at[peer], gathered.at[dof], sem_scatter, off, (pair, peer)))
+    gathered[dof] = local[dof]
+    for copy in copies:
+        copy.wait()
+    sums[...] = jnp.sum(gathered[...], axis=0)
+
+    copies = []
+    for off in range(1, pairs):
+        peer = lax.rem(pair + off, pairs)
+        copies.append(send(sums, crossed.at[pair], sem_cross, off, (peer, dof)))
+    crossed[pair] = sums[...]
+    for copy in copies:
+        copy.wait()
+    whole[dof] = jnp.sum(crossed[...], axis=0)
+
+    copies = []
+    for off in range(1, dofs):
+        peer = lax.rem(dof + off, dofs)
+        copies.append(send(whole.at[dof], whole.at[dof], sem_gather, off, (pair, peer)))
+    for copy in copies:
+        copy.wait()
+    gram_ref[...] = whole[...].reshape(gram_ref.shape)
+
+
+def apply_kernel(pairs, turn_ref, part_ref, out_ref, rotated, sem):
+    pair, dof = lax.axis_index("pair"), lax.axis_index("dof")
+    order = out_ref.shape[0]
+    quarter = part_ref.shape[1]
+    greet(pairs, 1, pair, dof)
+
+    def turned(place):
+        rows = pl.ds(pl.multiple_of(place * order, order), order)
+        return dot(turn_ref[rows, :], part_ref[...], (1, 0))
+
+    mine = pl.ds(pl.multiple_of(pair * quarter, quarter), quarter)
+    copies = []
+    for off in range(pairs - 1, 0, -1):
+        peer = lax.rem(pair + off, pairs)
+        rotated[off] = turned(peer)
+        copies.append(send(rotated.at[off], out_ref.at[:, mine], sem, off, (peer, dof)))
+    out_ref[:, mine] = turned(pair)
+    for copy in copies:
+        copy.wait()
+
+
+def in_vmem(count):
+    return [pl.BlockSpec(memory_space=pltpu.VMEM)] * count
+
+
 def body(snapshots):
-    order, dofs = snapshots.shape
-    pairs = lax.axis_size("pair")
-    part = lax.all_to_all(snapshots, "pair", split_axis=1, concat_axis=0, tiled=True)
-    gram = lax.psum(jnp.dot(part, part.T, precision=highest), ("pair", "dof"))
-    everything = lax.all_gather(snapshots, "pair", axis=0, tiled=True)
-    rows = pairs * order
+    order, dofs_here = snapshots.shape
+    pairs, dofs = lax.axis_size("pair"), lax.axis_size("dof")
+    rows, quarter = pairs * order, dofs_here // pairs
+    chunk = rows // dofs
+    f32 = jnp.float32
+    part, gram = pl.pallas_call(
+        functools.partial(gram_kernel, pairs, dofs),
+        out_shape=(
+            jax.ShapeDtypeStruct((rows, quarter), f32),
+            jax.ShapeDtypeStruct((rows, rows), f32),
+        ),
+        in_specs=in_vmem(1),
+        out_specs=tuple(in_vmem(2)),
+        scratch_shapes=[
+            pltpu.VMEM((dofs, chunk, rows), f32),
+            pltpu.VMEM((dofs, chunk, rows), f32),
+            pltpu.VMEM((chunk, rows), f32),
+            pltpu.VMEM((pairs, chunk, rows), f32),
+            pltpu.VMEM((dofs, chunk, rows), f32),
+            pltpu.SemaphoreType.DMA((2, pairs)),
+            pltpu.SemaphoreType.DMA((2, dofs)),
+            pltpu.SemaphoreType.DMA((2, pairs)),
+            pltpu.SemaphoreType.DMA((2, dofs)),
+        ],
+        compiler_params=pltpu.CompilerParams(
+            vmem_limit_bytes=32 * 2**20, collective_id=0, has_side_effects=True
+        ),
+        name="gram",
+    )(snapshots)
     turn = pl.pallas_call(
         functools.partial(kernel, pairs, order // 2),
-        out_shape=jax.ShapeDtypeStruct((rows, rows), jnp.float32),
-        in_specs=[pl.BlockSpec(memory_space=pltpu.VMEM)],
-        out_specs=pl.BlockSpec(memory_space=pltpu.VMEM),
+        out_shape=jax.ShapeDtypeStruct((rows, rows), f32),
+        in_specs=in_vmem(1),
+        out_specs=in_vmem(1)[0],
         compiler_params=pltpu.CompilerParams(vmem_limit_bytes=32 * 2**20),
-        cost_estimate=pl.CostEstimate(flops=10**9, bytes_accessed=10**8, transcendentals=0),
         name="rotations",
     )(gram)
-    mine = lax.dynamic_slice_in_dim(turn, lax.axis_index("pair") * order, order, 0)
-    return jnp.dot(mine, everything, precision=highest)
+    return pl.pallas_call(
+        functools.partial(apply_kernel, pairs),
+        out_shape=jax.ShapeDtypeStruct((order, dofs_here), f32),
+        in_specs=in_vmem(2),
+        out_specs=in_vmem(1)[0],
+        scratch_shapes=[
+            pltpu.VMEM((pairs, order, quarter), f32),
+            pltpu.SemaphoreType.DMA((2, pairs)),
+        ],
+        compiler_params=pltpu.CompilerParams(
+            vmem_limit_bytes=32 * 2**20, collective_id=1, has_side_effects=True
+        ),
+        name="apply",
+    )(turn, part)
 
 
 def solution(mesh):

time: 287 us -> 123 us (0.43)
  waiting for transfers between devices: 176 us -> 0 us
  Pallas kernels: 53.1 us -> 121 us
  blocking collectives: 31.8 us -> 0 us
  between operations: 14.9 us -> 0.02 us
  matrix products: 7.01 us -> 0 us
    psum x1 -> x0, waiting for transfers between devices: 176 us -> none  [body(): gram = lax.psum(jnp.dot(part, part.T, precision=highest), ('pair', 'dof'))]
    pallas_call x0 -> x2, Pallas kernels: none -> 67.8 us  [the longest x1 39.9 us: body(): pl.pallas_call(functools.partial(gram_kernel, pairs, dofs), out_shape=(ja...]
    all_to_all x1 -> x0, blocking collectives: 31.8 us -> none  [body(): lax.all_to_all(snapshots, 'pair', split_axis=1, concat_axis=0, tiled=True)]
    dot_general x2 -> x0, matrix products: 7.01 us -> none  [the longest x1 5.4 us: body(): return jnp.dot(mine, everything, precision=highest)]
  transfers between devices with their start and end apart: 2 -> 0, of which waited for: 1 -> 0; matrix products, arithmetic and copies ran while one was open for 0% -> 0% of each run, Pallas kernels for 19% -> 0%
where the time goes in v2:
time: 123 us
  Pallas kernels  121 us (98%)
  local copies, waits for them, and re-layouts  2.2 us (2%)
    pallas_call x1, Pallas kernels, body(): pl.pallas_call(functools.partial(kernel, pairs, order // 2), out_shape=ja...  53.1 us
    pallas_call x1, Pallas kernels, body(): pl.pallas_call(functools.partial(gram_kernel, pairs, dofs), out_shape=(ja...  39.9 us
    pallas_call x1, Pallas kernels, body(): pl.pallas_call(functools.partial(apply_kernel, pairs), out_shape=jax.Shap...  27.9 us

profile of v2, /device:TPU:0, one launch (start us, length us, event | category | flops | bytes accessed | tf_op | source)
XLA Modules:
  0.0 123.1 jit_solution(792990496534744941)
XLA Ops:
  0.0 0.0 copy-start
  0.0 1.2 copy-done
  1.2 39.9 %gram.1 = (f32[128,2048]{1,0:T(8,128)S(1)}, f32[128,128]{1,0:T(8,128)S(1)}) custom-call(f32[32,8192]{1,0:T(8,128)S(1)} %copy-done), custom_call_target="tpu_custom_call" | custom-call | tf_op jit(solution)/shard_map/gram/pallas_call | solution.py:295
  41.1 53.1 %rotations.1.turn_ref = f32[128,128]{1,0:T(8,128)S(1)} custom-call(f32[128,128]{1,0:T(8,128)S(1)} %get-tuple-element.7.gram_ref), custom_call_target="tpu_custom_call" | custom-call | tf_op jit(solution)/shard_map/rotations/pallas_call | solution.py:319
  94.2 27.9 %apply.1 = f32[32,8192]{1,0:T(8,128)S(1)} custom-call(f32[128,128]{1,0:T(8,128)S(1)} %rotations.1.turn_ref, f32[128,2048]{1,0:T(8,128)S(1)} %get-tuple-element.8.part_ref), custom_call_target="tpu_custom_call" | custom-call | tf_op jit(solution)/shard_map/apply/pallas_call | solution.py:327
  122.1 1.0 copy.3
Async XLA Ops:
  0.0 1.2 copy-start

commit v3 on v2

--- a/solution.py
+++ b/solution.py
@@ -74,6 +74,8 @@
     k0, kend = k_lane == 0, k_lane == half - 1
     r0, rend = row == 0, row == half - 1
     row_index = group_start + row
+    top_from = group_start + jnp.where(r0 | rend, row, row + 1)
+    low_from = group_start + jnp.where(r0, 1, row - 1)
     lane_q = lax.broadcasted_iota(jnp.int32, (order, LANES), 1) % half
     row_q = lax.broadcasted_iota(jnp.int32, (order, LANES), 0)
     q0, qend = lane_q == 0, lane_q == half - 1
@@ -108,25 +110,29 @@
         return jnp.where(r0, top, jnp.where(rend, low, up)), jnp.where(r0, up, down)
 
     def one_round(r, states):
-        m = r % circle
-        t_index, b_index = (m + k_lane) % circle, (m - k_lane + circle) % circle
-        swapped = k0 | (t_index > b_index)
+        m = jnp.where(r >= circle, r - circle, r)
+        t_index, b_index = m + row, m - row
+        t_index = jnp.where(t_index >= circle, t_index - circle, t_index)
+        b_index = jnp.where(b_index < 0, b_index + circle, b_index)
+        swapped = r0 | (t_index > b_index)
         threshold = jnp.where(swapped, jnp.float32(1.2e-38), jnp.float32(0.0))
         out = []
-        for aa, bb, ee, dd, qt, qb in states:
-            def pick(x):
-                s = jnp.sum(jnp.where(diagonal, x, 0.0), axis=0, keepdims=True)
-                return jnp.broadcast_to(s, x.shape)
-
-            co_j, si_j = angles(pick(aa), pick(dd), pick(bb), threshold)
-            co_i = jnp.take_along_axis(co_j, row_index, axis=1)
-            si_i = jnp.take_along_axis(si_j, row_index, axis=1)
-            ac, ad = aa * co_j - bb * si_j, aa * si_j + bb * co_j
-            ec, ed = ee * co_j - dd * si_j, ee * si_j + dd * co_j
-            a1, e1 = co_i * ac - si_i * ec, si_i * ac + co_i * ec
-            b1, d1 = co_i * ad - si_i * ed, si_i * ad + co_i * ed
+        for aa, bb, ee, dd, qt, qb, a_i, d_i, b_i in states:
+            def by_lane(x):
+                total = jnp.sum(jnp.where(diagonal, x, 0.0), axis=0, keepdims=True)
+                return jnp.broadcast_to(total, x.shape)
+
+            co_i, si_i = angles(a_i, d_i, b_i, threshold)
+            co_j, si_j = by_lane(co_i), by_lane(si_i)
+            a0, e0 = co_i * aa - si_i * ee, si_i * aa + co_i * ee
+            b0, d0 = co_i * bb - si_i * dd, si_i * bb + co_i * dd
+            a1, b1 = a0 * co_j - b0 * si_j, a0 * si_j + b0 * co_j
+            e1, d1 = e0 * co_j - d0 * si_j, e0 * si_j + d0 * co_j
             a2, e2 = row_shift(a1, e1)
             b2, d2 = row_shift(b1, d1)
+            a_i = jnp.take_along_axis(jnp.where(rend, b2, a2), top_from, axis=1)
+            d_i = jnp.take_along_axis(jnp.where(r0, e2, d2), low_from, axis=1)
+            b_i = jnp.take_along_axis(jnp.where(r0, a2, b2), low_from, axis=1)
             a3, b3 = column_shift(a2, b2, k0, kend)
             e3, d3 = column_shift(e2, d2, k0, kend)
             co_q = jnp.concatenate([co_j, co_j], axis=0)
@@ -134,7 +140,7 @@
             q1, q2 = column_shift(
                 qt * co_q - qb * si_q, qt * si_q + qb * co_q, q0, qend
             )
-            out.append((a3, b3, e3, d3, q1, q2))
+            out.append((a3, b3, e3, d3, q1, q2, a_i, d_i, b_i))
         return tuple(out)
 
     def blocks(gram, g):
@@ -154,7 +160,8 @@
         dd = jnp.where(unused, jnp.where(diagonal, spare + half, 0.0), gather(width, width))
         qt = jnp.where(row_q == lane_q, 1.0, 0.0).astype(f32)
         qb = jnp.where(row_q == lane_q + half, 1.0, 0.0).astype(f32)
-        return aa, bb, ee, dd, qt, qb
+        ends = [jnp.take_along_axis(x, row_index, axis=1) for x in (aa, dd, bb)]
+        return aa, bb, ee, dd, qt, qb, *ends
 
     def spread(states):
         place_row = lax.broadcasted_iota(jnp.int32, (width, LANES), 0) // half
@@ -176,7 +183,7 @@
     total = None
     for step in range(STEPS):
         states = tuple(blocks(gram, g) for g in range(groups))
-        states = lax.fori_loop(0, SWEEPS * circle, one_round, states)
+        states = lax.fori_loop(0, SWEEPS * circle, one_round, states, unroll=2)
         turn = dot(spread(states), to_next if step < STEPS - 1 else to_end, (1, 0))
         total = dot(enter, turn, (1, 0)) if total is None else dot(total, turn, (1, 0))
         if step < STEPS - 1:
@@ -208,7 +215,7 @@
     return copy
 
 
-def gram_kernel(pairs, dofs, x_ref, part_ref, gram_ref, local, gathered, sums, crossed, whole,
+def gram_kernel(pairs, dofs, x_ref, part_ref, gram_ref, early, local, gathered, sums, crossed, whole,
                 sem_x, sem_scatter, sem_cross, sem_gather):
     pair, dof = lax.axis_index("pair"), lax.axis_index("dof")
     order = x_ref.shape[0]
@@ -223,16 +230,22 @@
         return pl.ds(pl.multiple_of(place * quarter, quarter), quarter)
 
     copies = []
-    for off in range(pairs - 1, 0, -1):
-        peer = lax.rem(pair + off, pairs)
-        copies.append(send(
-            x_ref.at[:, columns_of(peer)], part_ref.at[rows_of(pair), :], sem_x, off, (peer, dof)
-        ))
-    part_ref[rows_of(pair), :] = x_ref[:, columns_of(pair)]
-    for copy in copies:
+    for which, held in ((0, early), (1, part_ref)):
+        for off in range(pairs - 1, 0, -1):
+            peer = lax.rem(pair + off, pairs)
+            copies.append(send(
+                x_ref.at[:, columns_of(which * pairs + peer)], held.at[rows_of(pair), :],
+                sem_x.at[which], off, (peer, dof),
+            ))
+        held[rows_of(pair), :] = x_ref[:, columns_of(which * pairs + pair)]
+    for copy in copies[:pairs - 1]:
+        copy.wait()
+    part = early[...]
+    gram = dot(part, part, (1, 1))
+    for copy in copies[pairs - 1:]:
         copy.wait()
     part = part_ref[...]
-    local[...] = dot(part, part, (1, 1)).reshape(local.shape)
+    local[...] = (gram + dot(part, part, (1, 1))).reshape(local.shape)
 
     copies = []
     for off in range(1, dofs):
@@ -261,7 +274,7 @@
     gram_ref[...] = whole[...].reshape(gram_ref.shape)
 
 
-def apply_kernel(pairs, turn_ref, part_ref, out_ref, rotated, sem):
+def apply_kernel(pairs, turn_ref, part_ref, all_ref, out_ref, rotated, sem):
     pair, dof = lax.axis_index("pair"), lax.axis_index("dof")
     order = out_ref.shape[0]
     quarter = part_ref.shape[1]
@@ -269,15 +282,16 @@
 
     def turned(place):
         rows = pl.ds(pl.multiple_of(place * order, order), order)
-        return dot(turn_ref[rows, :], part_ref[...], (1, 0))
-
-    mine = pl.ds(pl.multiple_of(pair * quarter, quarter), quarter)
+        return turn_ref[rows, :]
+
+    mine = pl.ds(pl.multiple_of((pairs + pair) * quarter, quarter), quarter)
     copies = []
     for off in range(pairs - 1, 0, -1):
         peer = lax.rem(pair + off, pairs)
-        rotated[off] = turned(peer)
+        rotated[off] = dot(turned(peer), part_ref[...], (1, 0))
         copies.append(send(rotated.at[off], out_ref.at[:, mine], sem, off, (peer, dof)))
-    out_ref[:, mine] = turned(pair)
+    out_ref[:, mine] = dot(turned(pair), part_ref[...], (1, 0))
+    out_ref[:, :pairs * quarter] = dot(turned(pair), all_ref[...], (1, 0))
     for copy in copies:
         copy.wait()
 
@@ -289,24 +303,25 @@
 def body(snapshots):
     order, dofs_here = snapshots.shape
     pairs, dofs = lax.axis_size("pair"), lax.axis_size("dof")
-    rows, quarter = pairs * order, dofs_here // pairs
+    rows, piece = pairs * order, dofs_here // (2 * pairs)
     chunk = rows // dofs
     f32 = jnp.float32
     part, gram = pl.pallas_call(
         functools.partial(gram_kernel, pairs, dofs),
         out_shape=(
-            jax.ShapeDtypeStruct((rows, quarter), f32),
+            jax.ShapeDtypeStruct((rows, piece), f32),
             jax.ShapeDtypeStruct((rows, rows), f32),
         ),
         in_specs=in_vmem(1),
         out_specs=tuple(in_vmem(2)),
         scratch_shapes=[
+            pltpu.VMEM((rows, piece), f32),
             pltpu.VMEM((dofs, chunk, rows), f32),
             pltpu.VMEM((dofs, chunk, rows), f32),
             pltpu.VMEM((chunk, rows), f32),
             pltpu.VMEM((pairs, chunk, rows), f32),
             pltpu.VMEM((dofs, chunk, rows), f32),
-            pltpu.SemaphoreType.DMA((2, pairs)),
+            pltpu.SemaphoreType.DMA((2, 2, pairs)),
             pltpu.SemaphoreType.DMA((2, dofs)),
             pltpu.SemaphoreType.DMA((2, pairs)),
             pltpu.SemaphoreType.DMA((2, dofs)),
@@ -316,28 +331,31 @@
         ),
         name="gram",
     )(snapshots)
+    gram, early = lax.optimization_barrier((gram, snapshots[:, :dofs_here // 2]))
+    everything = lax.all_gather(early, "pair", axis=0, tiled=True)
     turn = pl.pallas_call(
         functools.partial(kernel, pairs, order // 2),
         out_shape=jax.ShapeDtypeStruct((rows, rows), f32),
         in_specs=in_vmem(1),
         out_specs=in_vmem(1)[0],
         compiler_params=pltpu.CompilerParams(vmem_limit_bytes=32 * 2**20),
+        cost_estimate=pl.CostEstimate(flops=10**9, bytes_accessed=10**8, transcendentals=0),
         name="rotations",
     )(gram)
     return pl.pallas_call(
         functools.partial(apply_kernel, pairs),
         out_shape=jax.ShapeDtypeStruct((order, dofs_here), f32),
-        in_specs=in_vmem(2),
+        in_specs=in_vmem(3),
         out_specs=in_vmem(1)[0],
         scratch_shapes=[
-            pltpu.VMEM((pairs, order, quarter), f32),
+            pltpu.VMEM((pairs, order, piece), f32),
             pltpu.SemaphoreType.DMA((2, pairs)),
         ],
         compiler_params=pltpu.CompilerParams(
             vmem_limit_bytes=32 * 2**20, collective_id=1, has_side_effects=True
         ),
         name="apply",
-    )(turn, part)
+    )(turn, part, everything)
 
 
 def solution(mesh):

time: 123 us -> 120 us (0.976)
  Pallas kernels: 121 us -> 92.2 us
  between operations: 0.02 us -> 13.4 us
  waiting for transfers between devices: 0 us -> 8.9 us
  local copies, waits for them, and re-layouts: 2.2 us -> 5.66 us
    pallas_call x1, Pallas kernels: 53.1 us -> 37.3 us  [body(): pl.pallas_call(functools.partial(kernel, pairs, order // 2), out_shape=ja...]
    pallas_call x1, Pallas kernels: 27.9 us -> 15 us  [body(): pl.pallas_call(functools.partial(apply_kernel, pairs), out_shape=jax.Shap...]
    all_gather x0 -> x1, waiting for transfers between devices: none -> 8.88 us  [body(): everything = lax.all_gather(early, 'pair', axis=0, tiled=True)]
    slice x0 -> x1, local copies, waits for them, and re-layouts: none -> 1.87 us  [body(): snapshots[:, :dofs_here // 2]]
    unnamed x3 -> x5, local copies, waits for them, and re-layouts: 2.2 us -> 3.79 us
  transfers between devices with their start and end apart: 0 -> 1, of which waited for: 0 -> 1; matrix products, arithmetic and copies ran while one was open for 0% -> 0% of each run, Pallas kernels for 0% -> 31%
where the time goes in v3:
time: 120 us
  Pallas kernels  92.2 us (77%)
  between operations  13.4 us (11%)
  waiting for transfers between devices  8.9 us (7%)
  local copies, waits for them, and re-layouts  5.66 us (5%)
    pallas_call x1, Pallas kernels, body(): pl.pallas_call(functools.partial(gram_kernel, pairs, dofs), out_shape=(ja...  40 us
    pallas_call x1, Pallas kernels, body(): pl.pallas_call(functools.partial(kernel, pairs, order // 2), out_shape=ja...  37.3 us
    pallas_call x1, Pallas kernels, body(): pl.pallas_call(functools.partial(apply_kernel, pairs), out_shape=jax.Shap...  15 us
    all_gather x1, waiting for transfers between devices, body(): everything = lax.all_gather(early, 'pair', axis=0, tiled=True)  8.88 us
    unnamed x5, local copies, waits for them, and re-layouts  3.79 us
  transfers between devices with their start and end apart: 1, of which 1 were waited for; matrix products, arithmetic and copies ran while one was open for 0% of the time, Pallas kernels for 31%

profile of v3, /device:TPU:0, one launch (start us, length us, event | category | flops | bytes accessed | tf_op | source)
XLA Modules:
  0.0 120.2 jit_solution(3808693785479635694)
XLA Ops:
  6.5 0.0 all-gather.2.cloned.1.call-start
  6.5 1.9 %slice.3 = f32[32,4096]{1,0:T(8,128)} slice(f32[32,8192]{1,0:T(8,128)} %x_ref.1), slice={[0:32], [0:4096]} | slice | bytes 1048576 | tf_op jit(solution)/shard_map/slice | solution.py:334
  8.4 0.0 copy-start
  8.4 1.2 %copy-done = f32[32,8192]{1,0:T(8,128)S(1)} copy-done((f32[32,8192]{1,0:T(8,128)S(1)}, f32[32,8192]{1,0:T(8,128)}, u32[]{:S(2)}) %copy-start) | copy-done | bytes 1048600
  9.6 40.0 %gram.1 = (f32[128,1024]{1,0:T(8,128)S(1)}, f32[128,128]{1,0:T(8,128)S(1)}) custom-call(f32[32,8192]{1,0:T(8,128)S(1)} %copy-done), custom_call_target="tpu_custom_call" | custom-call | tf_op jit(solution)/shard_map/gram/pallas_call | solution.py:309
  49.6 0.0 all-gather.2.cloned.1.call-update
  49.6 37.3 %rotations.1.turn_ref = f32[128,128]{1,0:T(8,128)S(1)} custom-call(f32[128,128]{1,0:T(8,128)S(1)} %get-tuple-element.10.gram_ref), custom_call_target="tpu_custom_call" | custom-call | flops 1000000000 | bytes 100000000 | tf_op jit(solution)/shard_map/rotations/pallas_call | solution.py:336
  86.9 8.9 %all-gather.2.cloned.1.call-done.all_ref = f32[128,4096]{1,0:T(8,128)} async-done(((f32[32,4096]{1,0:T(8,128)}), f32[128,4096]{1,0:T(8,128)}) %all-gather.2.cloned.1.call-update) | async-done | bytes 2097168 | tf_op jit(solution)/shard_map/all_gather | solution.py:335
  95.8 0.0 copy-start.1
  95.8 1.6 %copy-done.1 = f32[128,4096]{1,0:T(8,128)S(1)} copy-done((f32[128,4096]{1,0:T(8,128)S(1)}, f32[128,4096]{1,0:T(8,128)}, u32[]{:S(2)}) %copy-start.1) | copy-done | bytes 2097176
  97.4 15.0 %apply.1 = f32[32,8192]{1,0:T(8,128)S(1)} custom-call(f32[128,128]{1,0:T(8,128)S(1)} %rotations.1.turn_ref, f32[128,1024]{1,0:T(8,128)S(1)} %get-tuple-element.11.part_ref, f32[128,4096]{1,0:T(8,128)S(1)} %copy-done.1), custom_call_target="tpu_custom_call" | custom-call | tf_op jit(solution)/shard_map/apply/pallas_call | solution.py:345
  112.4 1.0 copy.3
Async XLA Ops:
  6.5 89.2 %all-gather.2.cloned.1.call-start = ((), (), s32[]{:S(2)}) async-start(), calls=%async_computation | async-start | bytes 2621440 | tf_op jit(solution)/shard_map/all_gather | solution.py:335
  8.4 1.2 %copy-start = (f32[32,8192]{1,0:T(8,128)S(1)}, f32[32,8192]{1,0:T(8,128)}, u32[]{:S(2)}) copy-start(f32[32,8192]{1,0:T(8,128)} %x_ref.1) | copy-start | bytes 3145732
  95.8 1.6 %copy-start.1 = (f32[128,4096]{1,0:T(8,128)S(1)}, f32[128,4096]{1,0:T(8,128)}, u32[]{:S(2)}) copy-start(f32[128,4096]{1,0:T(8,128)} %all-gather.2.cloned.1.call-done.all_ref) | copy-start | bytes 6291460
Sparse Core Ops, SparseCore 0:
  49.8 45.9 all-gather.1

commit v4 on v3

--- a/solution.py
+++ b/solution.py
@@ -215,29 +215,33 @@
     return copy
 
 
-def gram_kernel(pairs, dofs, x_ref, part_ref, gram_ref, early, local, gathered, sums, crossed, whole,
+def gram_kernel(pairs, dofs, x_ref, part_ref, gram_ref, first_ref, early, local, gathered, sums, crossed, whole,
                 sem_x, sem_scatter, sem_cross, sem_gather):
     pair, dof = lax.axis_index("pair"), lax.axis_index("dof")
     order = x_ref.shape[0]
-    quarter = part_ref.shape[1]
-    chunk = sums.shape[0]
+    early_width, late_width = early.shape[1], part_ref.shape[1]
     greet(pairs, dofs, pair, dof)
 
     def rows_of(place):
         return pl.ds(pl.multiple_of(place * order, order), order)
 
-    def columns_of(place):
-        return pl.ds(pl.multiple_of(place * quarter, quarter), quarter)
-
-    copies = []
-    for which, held in ((0, early), (1, part_ref)):
+    def early_columns(place):
+        return pl.ds(pl.multiple_of(place * early_width, LANES), early_width)
+
+    def late_columns(place):
+        at = pairs * early_width + place * late_width
+        return pl.ds(pl.multiple_of(at, LANES), late_width)
+
+    copies = []
+    for which, held, columns in ((0, early, early_columns), (1, part_ref, late_columns)):
         for off in range(pairs - 1, 0, -1):
             peer = lax.rem(pair + off, pairs)
             copies.append(send(
-                x_ref.at[:, columns_of(which * pairs + peer)], held.at[rows_of(pair), :],
+                x_ref.at[:, columns(peer)], held.at[rows_of(pair), :],
                 sem_x.at[which], off, (peer, dof),
             ))
-        held[rows_of(pair), :] = x_ref[:, columns_of(which * pairs + pair)]
+        held[rows_of(pair), :] = x_ref[:, columns(pair)]
+    first_ref[...] = x_ref[:, :pairs * early_width]
     for copy in copies[:pairs - 1]:
         copy.wait()
     part = early[...]
@@ -274,7 +278,8 @@
     gram_ref[...] = whole[...].reshape(gram_ref.shape)
 
 
-def apply_kernel(pairs, turn_ref, part_ref, all_ref, out_ref, rotated, sem):
+def apply_kernel(pairs, turn_ref, part_ref, *refs):
+    *shifted, out_ref, rotated, everything, sem = refs
     pair, dof = lax.axis_index("pair"), lax.axis_index("dof")
     order = out_ref.shape[0]
     quarter = part_ref.shape[1]
@@ -284,14 +289,18 @@
         rows = pl.ds(pl.multiple_of(place * order, order), order)
         return turn_ref[rows, :]
 
-    mine = pl.ds(pl.multiple_of((pairs + pair) * quarter, quarter), quarter)
+    early_all = everything.shape[1]
+    mine = pl.ds(pl.multiple_of(early_all + pair * quarter, LANES), quarter)
     copies = []
     for off in range(pairs - 1, 0, -1):
         peer = lax.rem(pair + off, pairs)
         rotated[off] = dot(turned(peer), part_ref[...], (1, 0))
         copies.append(send(rotated.at[off], out_ref.at[:, mine], sem, off, (peer, dof)))
     out_ref[:, mine] = dot(turned(pair), part_ref[...], (1, 0))
-    out_ref[:, :pairs * quarter] = dot(turned(pair), all_ref[...], (1, 0))
+    for off, block in enumerate(shifted):
+        source = lax.rem(pair + pairs - off, pairs)
+        everything[pl.ds(pl.multiple_of(source * order, order), order), :] = block[...]
+    out_ref[:, :early_all] = dot(turned(pair), everything[...], (1, 0))
     for copy in copies:
         copy.wait()
 
@@ -303,19 +312,22 @@
 def body(snapshots):
     order, dofs_here = snapshots.shape
     pairs, dofs = lax.axis_size("pair"), lax.axis_size("dof")
-    rows, piece = pairs * order, dofs_here // (2 * pairs)
+    rows, share = pairs * order, dofs_here // pairs
+    early = max(share * 6 // 16 // LANES, 1) * LANES
+    late = share - early
     chunk = rows // dofs
     f32 = jnp.float32
-    part, gram = pl.pallas_call(
+    part, gram, first = pl.pallas_call(
         functools.partial(gram_kernel, pairs, dofs),
         out_shape=(
-            jax.ShapeDtypeStruct((rows, piece), f32),
+            jax.ShapeDtypeStruct((rows, late), f32),
             jax.ShapeDtypeStruct((rows, rows), f32),
+            jax.ShapeDtypeStruct((order, pairs * early), f32),
         ),
         in_specs=in_vmem(1),
-        out_specs=tuple(in_vmem(2)),
+        out_specs=tuple(in_vmem(3)),
         scratch_shapes=[
-            pltpu.VMEM((rows, piece), f32),
+            pltpu.VMEM((rows, early), f32),
             pltpu.VMEM((dofs, chunk, rows), f32),
             pltpu.VMEM((dofs, chunk, rows), f32),
             pltpu.VMEM((chunk, rows), f32),
@@ -331,8 +343,10 @@
         ),
         name="gram",
     )(snapshots)
-    gram, early = lax.optimization_barrier((gram, snapshots[:, :dofs_here // 2]))
-    everything = lax.all_gather(early, "pair", axis=0, tiled=True)
+    shifted = [first] + [
+        lax.ppermute(first, "pair", [(i, (i + off) % pairs) for i in range(pairs)])
+        for off in range(1, pairs)
+    ]
     turn = pl.pallas_call(
         functools.partial(kernel, pairs, order // 2),
         out_shape=jax.ShapeDtypeStruct((rows, rows), f32),
@@ -345,17 +359,18 @@
     return pl.pallas_call(
         functools.partial(apply_kernel, pairs),
         out_shape=jax.ShapeDtypeStruct((order, dofs_here), f32),
-        in_specs=in_vmem(3),
+        in_specs=in_vmem(2 + pairs),
         out_specs=in_vmem(1)[0],
         scratch_shapes=[
-            pltpu.VMEM((pairs, order, piece), f32),
+            pltpu.VMEM((pairs, order, late), f32),
+            pltpu.VMEM((rows, pairs * early), f32),
             pltpu.SemaphoreType.DMA((2, pairs)),
         ],
         compiler_params=pltpu.CompilerParams(
             vmem_limit_bytes=32 * 2**20, collective_id=1, has_side_effects=True
         ),
         name="apply",
-    )(turn, part, everything)
+    )(turn, part, *shifted)
 
 
 def solution(mesh):

time: 120 us -> 103 us (0.86)
  between operations: 13.4 us -> 0.04 us
  waiting for transfers between devices: 8.9 us -> 0.01 us
  starting transfers between devices: 0.01 us -> 4.69 us
  local copies, waits for them, and re-layouts: 5.66 us -> 2.2 us
  Pallas kernels: 92.2 us -> 95.5 us
    all_gather x1 -> x0, waiting for transfers between devices: 8.88 us -> none  [body(): everything = lax.all_gather(early, 'pair', axis=0, tiled=True)]
    ppermute x0 -> x3, starting transfers between devices: none -> 4.69 us  [body(): lax.ppermute(first, 'pair', [(i, (i + off) % pairs) for i in range(pairs)])]
    pallas_call x1, Pallas kernels: 15 us -> 18.3 us  [body(): pl.pallas_call(functools.partial(apply_kernel, pairs), out_shape=jax.Shap...]
    slice x1 -> x0, local copies, waits for them, and re-layouts: 1.87 us -> none  [body(): snapshots[:, :dofs_here // 2]]
    unnamed x5 -> x3, local copies, waits for them, and re-layouts: 3.79 us -> 2.2 us
  transfers between devices with their start and end apart: 1 -> 3, of which waited for: 1 -> 0; matrix products, arithmetic and copies ran while one was open for 0% -> 0% of each run, Pallas kernels for 31% -> 36%
where the time goes in v4:
time: 103 us; the launch traced here: 102 us
  Pallas kernels  95.5 us (93%)
  starting transfers between devices  4.69 us (5%)
  local copies, waits for them, and re-layouts  2.2 us (2%)
    pallas_call x1, Pallas kernels, body(): pl.pallas_call(functools.partial(gram_kernel, pairs, dofs), out_shape=(ja...  39.9 us
    pallas_call x1, Pallas kernels, body(): pl.pallas_call(functools.partial(kernel, pairs, order // 2), out_shape=ja...  37.3 us
    pallas_call x1, Pallas kernels, body(): pl.pallas_call(functools.partial(apply_kernel, pairs), out_shape=jax.Shap...  18.3 us
    ppermute x3, starting transfers between devices, body(): lax.ppermute(first, 'pair', [(i, (i + off) % pairs) for i in range(pairs)])  4.69 us
    unnamed x3, local copies, waits for them, and re-layouts  2.2 us
  transfers between devices with their start and end apart: 3, of which 0 were waited for; matrix products, arithmetic and copies ran while one was open for 0% of the time, Pallas kernels for 36%

profile of v4, /device:TPU:0, one launch (start us, length us, event | category | flops | bytes accessed | tf_op | source)
XLA Modules:
  0.0 102.4 jit_solution(3201323358693783567)
XLA Ops:
  0.0 0.0 copy-start
  0.0 1.2 %copy-done = f32[32,8192]{1,0:T(8,128)S(1)} copy-done((f32[32,8192]{1,0:T(8,128)S(1)}, f32[32,8192]{1,0:T(8,128)}, u32[]{:S(2)}) %copy-start) | copy-done | bytes 1048600
  1.2 39.9 %gram.1 = (f32[128,1280]{1,0:T(8,128)S(1)}, f32[128,128]{1,0:T(8,128)S(1)}, f32[32,3072]{1,0:T(8,128)S(1)}) custom-call(f32[32,8192]{1,0:T(8,128)S(1)} %copy-done), custom_call_target="tpu_custom_call" | custom-call | tf_op jit(solution)/shard_map/gram/pallas_call | solution.py:320
  41.2 3.6 %collective-permute-start.2 = (f32[32,3072]{1,0:T(8,128)S(1)}, f32[32,3072]{1,0:T(8,128)S(1)}, u32[]{:S(2)}, u32[]{:S(2)}) collective-permute-start(f32[32,3072]{1,0:T(8,128)S(1)} %get-tuple-element.10.refs_0_), channel_id=1, source_target_pairs={{0,24},{8,0},{16,8},{24,16},{1,25},{9,1},{17,9},{25,17},{2,26},{10... | collective-permute-start | bytes 1179656 | tf_op jit(solution)/shard_map/ppermute | solution.py:347
  44.8 0.0 collective-permute-start.1
  44.8 1.0 %collective-permute-start = (f32[32,3072]{1,0:T(8,128)S(1)}, f32[32,3072]{1,0:T(8,128)S(1)}, u32[]{:S(2)}, u32[]{:S(2)}) collective-permute-start(f32[32,3072]{1,0:T(8,128)S(1)} %get-tuple-element.10.refs_0_), channel_id=1, source_target_pairs={{0,8},{8,16},{16,24},{24,0},{1,9},{9,17},{17,25},{25,1},{2,10},{10... | collective-permute-start | bytes 1179656 | tf_op jit(solution)/shard_map/ppermute | solution.py:347
  45.8 37.3 %rotations.1.turn_ref = f32[128,128]{1,0:T(8,128)S(1)} custom-call(f32[128,128]{1,0:T(8,128)S(1)} %get-tuple-element.8.gram_ref), custom_call_target="tpu_custom_call" | custom-call | flops 1000000000 | bytes 100000000 | tf_op jit(solution)/shard_map/rotations/pallas_call | solution.py:350
  83.1 0.0 collective-permute-done.2.refs_3_
  83.1 0.0 collective-permute-done.1.refs_2_
  83.1 0.0 collective-permute-done.refs_1_
  83.1 18.3 %apply.1 = f32[32,8192]{1,0:T(8,128)S(1)} custom-call(f32[128,128]{1,0:T(8,128)S(1)} %rotations.1.turn_ref, f32[128,1280]{1,0:T(8,128)S(1)} %get-tuple-element.9.part_ref, f32[32,3072]{1,0:T(8,128)S(1)} %get-tuple-element.10.refs_0_, f32[32,3072]{1,0:T(8,128)S(1)} %collective-permute-done.refs_1_, f32[32,3072]{1,0:T(8,128)S(1)} %collective-permute-done.1.refs_2_, ...), custom_call_target="tpu_custom_call" | custom-call | tf_op jit(solution)/shard_map/apply/pallas_call | solution.py:359
  101.5 1.0 copy.3
Async XLA Ops:
  0.0 1.2 %copy-start = (f32[32,8192]{1,0:T(8,128)S(1)}, f32[32,8192]{1,0:T(8,128)}, u32[]{:S(2)}) copy-start(f32[32,8192]{1,0:T(8,128)} %x_ref.1) | copy-start | bytes 3145732
  41.2 42.0 %collective-permute-start.2 = (f32[32,3072]{1,0:T(8,128)S(1)}, f32[32,3072]{1,0:T(8,128)S(1)}, u32[]{:S(2)}, u32[]{:S(2)}) collective-permute-start(f32[32,3072]{1,0:T(8,128)S(1)} %get-tuple-element.10.refs_0_), channel_id=1, source_target_pairs={{0,24},{8,0},{16,8},{24,16},{1,25},{9,1},{17,9},{25,17},{2,26},{10... | collective-permute-start | bytes 1179656 | tf_op jit(solution)/shard_map/ppermute | solution.py:347
  44.8 38.3 %collective-permute-start.1 = (f32[32,3072]{1,0:T(8,128)S(1)}, f32[32,3072]{1,0:T(8,128)S(1)}, u32[]{:S(2)}, u32[]{:S(2)}) collective-permute-start(f32[32,3072]{1,0:T(8,128)S(1)} %get-tuple-element.10.refs_0_), channel_id=1, source_target_pairs={{0,16},{8,24},{16,0},{24,8},{1,17},{9,25},{17,1},{25,9},{2,18},{10... | collective-permute-start | bytes 1179656 | tf_op jit(solution)/shard_map/ppermute | solution.py:347
  44.8 38.3 %collective-permute-start = (f32[32,3072]{1,0:T(8,128)S(1)}, f32[32,3072]{1,0:T(8,128)S(1)}, u32[]{:S(2)}, u32[]{:S(2)}) collective-permute-start(f32[32,3072]{1,0:T(8,128)S(1)} %get-tuple-element.10.refs_0_), channel_id=1, source_target_pairs={{0,8},{8,16},{16,24},{24,0},{1,9},{9,17},{17,25},{25,1},{2,10},{10... | collective-permute-start | bytes 1179656 | tf_op jit(solution)/shard_map/ppermute | solution.py:347
